TPU v7x, 1024 devices: a whole 4x4x32 slice. The times are simulated.
1024 devices in a mesh: section: 32 (over z_hi, y, core), expert: 32 (over z_lo, x).
Axes of the slice: x: 4, y: 4, z: 32 (z_hi: 4, z_lo: 8; z = z_hi * 8 + z_lo), core: 2. Of those that a mesh axis runs over, the one named last changes fastest.
Arguments:
- states: bfloat16 [32, 256, 3584], P('section', 'expert'), may hold values from -6 to 6
- norm_gain: float32 [32, 3584], P('section'), may hold values from 0.1 to 1.9
- router: bfloat16 [32, 3584, 4], P('section'), may hold values from -0.09375 to 0.09375
- w_gate: bfloat16 [32, 3584, 4096], P('section', None, 'expert'), may hold values from -0.09375 to 0.09375
- w_up: bfloat16 [32, 3584, 4096], P('section', None, 'expert'), may hold values from -0.09375 to 0.09375
- w_down: bfloat16 [32, 4096, 3584], P('section', 'expert'), may hold values from -0.1875 to 0.1875
- routes: int32 [2, 32, 256, 2], P(None, 'section', 'expert'), may hold values from 0 to 3, all different within a row; in each aligned block of 8 rows (0 to 7, 8 to 15, ..., all dimensions but the last counted through in order) at most 8 rows name the same one
Outputs:
- final_states: bfloat16 [32, 256, 3584], P('section', 'expert')
Inputs may be any that keep to these rules, and one draw needn't show every extreme that they name: `routes`: each token names 2 different experts. Within one tick and one section, among the 8 tokens of one index of the expert axis, no expert is named by more than 8 tokens; in some such blocks one expert is named by exactly 8.
All inputs are finite; a program needn't handle non-finite values.
Results may differ from a plain program's by a relative error of at most 0.0064.
Values may be sent and summed in bfloat16 or wider, within the bound.
A program may use at most 32 MiB of HBM per device.

v0:
```python
import jax
import jax.numpy as jnp
from jax import lax
from jax.sharding import PartitionSpec as P

TICKS = 2


EPSILON = 1e-06


def passed_along(value, axis, steps):
    count = lax.axis_size(axis)
    pairs = [(source, (source + steps) % count) for source in range(count)]
    return lax.ppermute(value, axis, pairs)


def normalize(states, gain):
    values = states.astype(jnp.float32)
    meansq = jnp.mean(values * values, axis=-1, keepdims=True)
    return (values * lax.rsqrt(meansq + EPSILON) * gain).astype(jnp.bfloat16)


def slot_positions(expert_ids, experts, sources):
    onehot = (expert_ids[:, :, None] == jnp.arange(experts, dtype=jnp.int32)).astype(jnp.int32)
    named = jnp.sum(onehot, axis=1)
    grouped = named.reshape(sources, -1, experts)
    before = (jnp.cumsum(grouped, axis=1) - grouped).reshape(-1, experts)
    position = jnp.sum(onehot * before[:, None, :], axis=2)
    return (onehot, position)


def gate_values(normed, router, onehot):
    logits = jnp.dot(normed, router, preferred_element_type=jnp.float32)
    affinity = jax.nn.sigmoid(logits)
    chosen = jnp.sum(onehot.astype(jnp.float32) * affinity[:, None, :], axis=2)
    return chosen / jnp.sum(chosen, axis=1, keepdims=True)


def on_device(states, norm_gain, router, w_gate, w_up, w_down, routes):
    devices = lax.axis_size("expert")
    experts = router.shape[2]
    shards = devices // experts
    tok_rows = states.shape[1]
    top_count = routes.shape[3]
    width = states.shape[2]
    capacity = min(tok_rows, 2 * tok_rows * top_count // experts)
    gate_local = w_gate[0]
    lift_local = w_up[0]
    down_local = w_down[0]
    current = states
    for tick_index in range(TICKS):
        expert_ids = routes[tick_index, 0]
        normed = normalize(current[0], norm_gain[0])
        onehot, position = slot_positions(expert_ids, experts, 1)
        gates = gate_values(normed, router[0], onehot)
        slot_index = expert_ids * capacity + position
        place = (slot_index[:, :, None] == jnp.arange(experts * capacity, dtype=jnp.int32)).astype(
            jnp.bfloat16
        )
        packed = jnp.einsum("tks,td->sd", place, normed, preferred_element_type=jnp.float32).astype(
            jnp.bfloat16
        )
        outgoing = jnp.broadcast_to(
            packed.reshape(experts, 1, capacity, width), (experts, shards, capacity, width)
        )
        outgoing = outgoing.reshape(devices, capacity, width)
        buffer = lax.all_to_all(outgoing, "expert", split_axis=0, concat_axis=0, tiled=True)
        count = buffer.shape[1]
        flat_rows = buffer.reshape(devices * count, width)
        gate_out = jnp.dot(flat_rows, gate_local, preferred_element_type=jnp.float32)
        lifted = jnp.dot(flat_rows, lift_local, preferred_element_type=jnp.float32)
        hidden = (jax.nn.silu(gate_out) * lifted).astype(jnp.bfloat16)
        partial_value = jnp.dot(hidden, down_local, preferred_element_type=jnp.float32).astype(
            jnp.bfloat16
        )
        returned = lax.all_to_all(
            partial_value.reshape(devices, count, width),
            "expert",
            split_axis=0,
            concat_axis=0,
            tiled=True,
        )
        summed = jnp.sum(
            returned.astype(jnp.float32).reshape(experts, shards, capacity, width), axis=1
        )
        summed = summed.reshape(experts * capacity, width)
        picked = jnp.einsum(
            "tks,sd->tkd", place.astype(jnp.float32), summed, precision=lax.Precision.HIGHEST
        )
        mixed = jnp.sum(picked * gates[:, :, None], axis=1)
        updated = (current[0].astype(jnp.float32) + mixed).astype(jnp.bfloat16)
        current = passed_along(updated[None], "section", 1)
    return current


def solution(mesh):
    placed = (
        P("section", "expert", None),
        P("section", None),
        P("section", None, None),
        P("section", None, "expert"),
        P("section", None, "expert"),
        P("section", "expert", None),
        P(None, "section", "expert", None),
    )
    return jax.shard_map(
        on_device,
        mesh=mesh,
        in_specs=placed,
        out_specs=P("section", "expert", None),
        check_vma=False,
    )
```

profile of v0, /device:TPU:6, one launch (start us, length us, event | category | flops | bytes accessed | tf_op | source)
XLA Modules:
  0.0 413.2 jit_solution(8376012622880990064)
XLA Ops:
  0.0 1.0 fusion.63
  1.1 0.7 slice_bitcast_fusion
  1.8 0.2 reduce_window_sum.18
  2.0 0.2 reduce_window_sum.17
  2.2 0.7 multiply_add_fusion
  3.0 0.8 reduce.2
  3.7 1.1 fusion.2
  4.8 0.1 broadcast_in_dim.9
  5.0 99.9 %all_to_all.20 = bf16[32,8,3584]{2,1,0:T(8,128)(2,1)S(1)} all-to-all(bf16[32,8,3584]{2,1,0:T(8,128)(2,1)S(1)} %bitcast.116), channel_id=1, replica_groups=mesh['section'=32,'expert'=32] {'expert'}, dimensions={0} | all-to-all | bytes 3670016 | tf_op jit(solution)/shard_map/all_to_all | solution.py:68
  104.9 0.6 fusion.10
  105.5 3.6 fusion
  109.1 7.7 %all-to-all-start.1 = ((bf16[32,8,3584]{2,1,0:T(8,128)(2,1)}), bf16[32,8,3584]{2,1,0:T(8,128)(2,1)S(1)}, u32[]{:S(2)}, u32[]{:S(2)}) async-start(bf16[32,8,3584]{2,1,0:T(8,128)(2,1)} %fusion), calls=%async_computation.1 | async-start | bytes 3670016 | tf_op jit(solution)/shard_map/all_to_all | solution.py:77
  116.8 0.2 fusion.31
  117.1 83.5 %all-to-all-done.1 = bf16[32,8,3584]{2,1,0:T(8,128)(2,1)S(1)} async-done(((bf16[32,8,3584]{2,1,0:T(8,128)(2,1)}), bf16[32,8,3584]{2,1,0:T(8,128)(2,1)S(1)}, u32[]{:S(2)}, u32[]{:S(2)}) %all-to-all-start.1) | async-done | bytes 1835040 | tf_op jit(solution)/shard_map/all_to_all | solution.py:77
  200.6 0.3 convert_reduce_fusion.1
  200.9 0.3 fusion.12
  201.2 1.9 collective-permute-start
  203.2 16.4 %collective-permute-done = bf16[1,8,3584]{2,1,0:T(8,128)(2,1)S(1)} collective-permute-done((bf16[1,8,3584]{2,1,0:T(8,128)(2,1)S(1)}, bf16[1,8,3584]{2,1,0:T(8,128)(2,1)S(1)}, u32[]{:S(2)}, u32[]{:S(2)}) %collective-permute-start) | collective-permute-done | bytes 57376 | tf_op jit(solution)/shard_map/ppermute | solution.py:15
  219.7 0.1 fusion.60
  219.8 0.3 fusion.3
  220.1 0.1 broadcast_in_dim.11
  220.2 78.6 %all_to_all.21 = bf16[32,8,3584]{2,1,0:T(8,128)(2,1)S(1)} all-to-all(bf16[32,8,3584]{2,1,0:T(8,128)(2,1)S(1)} %bitcast.117), channel_id=1, replica_groups=mesh['section'=32,'expert'=32] {'expert'}, dimensions={0} | all-to-all | bytes 3670016 | tf_op jit(solution)/shard_map/all_to_all | solution.py:68
  298.8 0.6 fusion.6
  299.5 3.6 fusion.1
  303.1 7.5 %all-to-all-start.3 = ((bf16[32,8,3584]{2,1,0:T(8,128)(2,1)}), bf16[32,8,3584]{2,1,0:T(8,128)(2,1)S(1)}, u32[]{:S(2)}, u32[]{:S(2)}) async-start(bf16[32,8,3584]{2,1,0:T(8,128)(2,1)} %fusion.1), calls=%async_computation.3 | async-start | bytes 3670016 | tf_op jit(solution)/shard_map/all_to_all | solution.py:77
  310.6 0.2 fusion.28
  310.9 80.4 %all-to-all-done.3 = bf16[32,8,3584]{2,1,0:T(8,128)(2,1)S(1)} async-done(((bf16[32,8,3584]{2,1,0:T(8,128)(2,1)}), bf16[32,8,3584]{2,1,0:T(8,128)(2,1)S(1)}, u32[]{:S(2)}, u32[]{:S(2)}) %all-to-all-start.3) | async-done | bytes 1835040 | tf_op jit(solution)/shard_map/all_to_all | solution.py:77
  391.3 0.3 convert_reduce_fusion
  391.5 0.3 fusion.13
  391.9 1.9 collective-permute-start.1
  393.8 18.8 %collective-permute-done.1 = bf16[1,8,3584]{2,1,0:T(8,128)(2,1)S(1)} collective-permute-done((bf16[1,8,3584]{2,1,0:T(8,128)(2,1)S(1)}, bf16[1,8,3584]{2,1,0:T(8,128)(2,1)S(1)}, u32[]{:S(2)}, u32[]{:S(2)}) %collective-permute-start.1) | collective-permute-done | bytes 57376 | tf_op jit(solution)/shard_map/ppermute | solution.py:15
  412.6 0.6 copy.13
  (25 shorter events, 0.4 us)
Async XLA Ops:
  0.0 105.5 %copy-start = (bf16[1,128,3584]{2,1,0:T(8,128)(2,1)S(1)}, bf16[1,128,3584]{2,1,0:T(8,128)(2,1)}, u32[]{:S(2)}) copy-start(bf16[1,128,3584]{2,1,0:T(8,128)(2,1)} %param.12) | copy-start | bytes 2752516
  5.0 99.9 %copy-start.1 = (bf16[1,3584,128]{2,1,0:T(8,128)(2,1)S(1)}, bf16[1,3584,128]{2,1,0:T(8,128)(2,1)}, u32[]{:S(2)}) copy-start(bf16[1,3584,128]{2,1,0:T(8,128)(2,1)} %param.10) | copy-start | bytes 2752516
  109.1 7.7 %copy-start.3 = (bf16[1,8,3584]{2,1,0:T(8,128)(2,1)S(1)}, bf16[1,8,3584]{2,1,0:T(8,128)(2,1)}, u32[]{:S(2)}) copy-start(bf16[1,8,3584]{2,1,0:T(8,128)(2,1)} %param.7) | copy-start | bytes 172036
  109.1 7.7 %copy-start.4 = (bf16[1,3584,4]{1,2,0:T(4,128)(2,1)S(1)}, bf16[1,3584,4]{1,2,0:T(4,128)(2,1)}, u32[]{:S(2)}) copy-start(bf16[1,3584,4]{1,2,0:T(4,128)(2,1)} %param.9) | copy-start | bytes 86020
  109.1 91.5 %all-to-all-start.1 = ((bf16[32,8,3584]{2,1,0:T(8,128)(2,1)}), bf16[32,8,3584]{2,1,0:T(8,128)(2,1)S(1)}, u32[]{:S(2)}, u32[]{:S(2)}) async-start(bf16[32,8,3584]{2,1,0:T(8,128)(2,1)} %fusion), calls=%async_computation.1 | async-start | bytes 3670016 | tf_op jit(solution)/shard_map/all_to_all | solution.py:77
  201.2 18.4 %collective-permute-start = (bf16[1,8,3584]{2,1,0:T(8,128)(2,1)S(1)}, bf16[1,8,3584]{2,1,0:T(8,128)(2,1)S(1)}, u32[]{:S(2)}, u32[]{:S(2)}) collective-permute-start(bf16[1,8,3584]{2,1,0:T(8,128)(2,1)S(1)} %fusion.68), channel_id=1, source_target_pairs={{0,32},{32,64},{64,96},{96,128},{128,160},{160,192},{192,224},{224... | collective-permute-start | bytes 172040 | tf_op jit(solution)/shard_map/ppermute | solution.py:15
  220.2 78.6 %copy-start.2 = (bf16[1,3584,128]{2,1,0:T(8,128)(2,1)S(1)}, bf16[1,3584,128]{2,1,0:T(8,128)(2,1)}, u32[]{:S(2)}) copy-start(bf16[1,3584,128]{2,1,0:T(8,128)(2,1)} %param.10) | copy-start | bytes 2752516
  303.1 88.2 %all-to-all-start.3 = ((bf16[32,8,3584]{2,1,0:T(8,128)(2,1)}), bf16[32,8,3584]{2,1,0:T(8,128)(2,1)S(1)}, u32[]{:S(2)}, u32[]{:S(2)}) async-start(bf16[32,8,3584]{2,1,0:T(8,128)(2,1)} %fusion.1), calls=%async_computation.3 | async-start | bytes 3670016 | tf_op jit(solution)/shard_map/all_to_all | solution.py:77
  391.9 20.7 %collective-permute-start.1 = (bf16[1,8,3584]{2,1,0:T(8,128)(2,1)S(1)}, bf16[1,8,3584]{2,1,0:T(8,128)(2,1)S(1)}, u32[]{:S(2)}, u32[]{:S(2)}) collective-permute-start(bf16[1,8,3584]{2,1,0:T(8,128)(2,1)S(1)} %fusion.71), channel_id=1, source_target_pairs={{0,32},{32,64},{64,96},{96,128},{128,160},{160,192},{192,224},{224... | collective-permute-start | bytes 172040 | tf_op jit(solution)/shard_map/ppermute | solution.py:15
where the time goes:
time: 414 us; the launch traced here: 413 us
  waiting for transfers between devices  199 us (48%)
  blocking collectives  178 us (43%)
  starting transfers between devices  19 us (5%)
  matrix products  10.9 us (3%)
    all_to_all x2, blocking collectives, on_device(): lax.all_to_all(outgoing, 'expert', split_axis=0, concat_axis=0, tiled=True)  178 us
    all_to_all x2, waiting for transfers between devices, on_device(): lax.all_to_all(partial_value.reshape(devices, count, width), 'expert', sp...  164 us
    ppermute x2, waiting for transfers between devices, passed_along(): return lax.ppermute(value, axis, pairs)  35.2 us
    all_to_all x2, starting transfers between devices, on_device(): lax.all_to_all(partial_value.reshape(devices, count, width), 'expert', sp...  15.2 us
  transfers between devices with their start and end apart: 4, of which 4 were waited for; matrix products, arithmetic and copies ran while one was open for 0% of the time, Pallas kernels for 0%

commit v1 on v0

v1 whole, which is shorter than its diff:
```python
import jax
import jax.numpy as jnp
from jax import lax
from jax.sharding import PartitionSpec as P

TICKS = 2
EPSILON = 1e-06


def normalize(states, gain):
    values = states.astype(jnp.float32)
    meansq = jnp.mean(values * values, axis=-1, keepdims=True)
    return (values * lax.rsqrt(meansq + EPSILON) * gain).astype(jnp.bfloat16)


def dense_gates(normed, router, expert_ids):
    experts = router.shape[1]
    affinity = jax.nn.sigmoid(jnp.dot(normed, router, preferred_element_type=jnp.float32))
    named = jnp.any(expert_ids[:, :, None] == jnp.arange(experts, dtype=jnp.int32), axis=1)
    chosen = jnp.where(named, affinity, 0.0)
    return chosen / jnp.sum(chosen, axis=1, keepdims=True)


def on_device(states, norm_gain, router, w_gate, w_up, w_down, routes):
    devices = lax.axis_size("expert")
    experts = router.shape[2]
    shards = devices // experts
    width = states.shape[2]
    mine = lax.axis_index("expert") // shards
    current = states[0]
    sections = lax.axis_size("section")
    for tick in range(TICKS):
        normed = normalize(current, norm_gain[0])
        gates = dense_gates(normed, router[0], routes[tick, 0])
        high = gates.astype(jnp.bfloat16)
        low = (gates - high.astype(jnp.float32)).astype(jnp.bfloat16)
        block = jnp.concatenate(
            [normed, jnp.pad(jnp.concatenate([high, low], axis=1), ((0, 0), (0, 128 - 2 * experts)))],
            axis=1,
        )
        rows = lax.all_gather(block, "expert", axis=0, tiled=True)
        extra = rows[:, width:].astype(jnp.float32)
        picked = jnp.arange(128, dtype=jnp.int32) % experts == mine
        picked = picked & (jnp.arange(128, dtype=jnp.int32) < 2 * experts)
        gate = jnp.sum(jnp.where(picked, extra, 0.0), axis=1, keepdims=True)
        rows = rows[:, :width]
        gate_out = jnp.dot(rows, w_gate[0], preferred_element_type=jnp.float32)
        lifted = jnp.dot(rows, w_up[0], preferred_element_type=jnp.float32)
        hidden = (jax.nn.silu(gate_out) * lifted * gate).astype(jnp.bfloat16)
        partial = jnp.dot(hidden, w_down[0], preferred_element_type=jnp.float32).astype(jnp.bfloat16)
        mixed = lax.psum_scatter(partial, "expert", scatter_dimension=0, tiled=True)
        updated = (current.astype(jnp.float32) + mixed.astype(jnp.float32)).astype(jnp.bfloat16)
        current = lax.ppermute(updated, "section", [(s, (s + 1) % sections) for s in range(sections)])
    return current[None]


def solution(mesh):
    placed = (
        P("section", "expert", None),
        P("section", None),
        P("section", None, None),
        P("section", None, "expert"),
        P("section", None, "expert"),
        P("section", "expert", None),
        P(None, "section", "expert", None),
    )
    return jax.shard_map(
        on_device,
        mesh=mesh,
        in_specs=placed,
        out_specs=P("section", "expert", None),
        check_vma=False,
    )
```

time: 414 us -> 1030 us (2.49); the launches traced: 413 us -> 1020 us
  waiting for transfers between devices: 199 us -> 979 us
  blocking collectives: 178 us -> 0 us
  starting transfers between devices: 19 us -> 3.97 us
  between operations: 0.18 us -> 13.3 us
    reduce_scatter x0 -> x2, waiting for transfers between devices: none -> 487 us  [on_device(): mixed = lax.psum_scatter(partial, 'expert', scatter_dimension=0, tiled=True)]
    all_gather x0 -> x2, waiting for transfers between devices: none -> 463 us  [on_device(): rows = lax.all_gather(block, 'expert', axis=0, tiled=True)]
    all_to_all x2 -> x0, blocking collectives: 178 us -> none  [on_device(): lax.all_to_all(outgoing, 'expert', split_axis=0, concat_axis=0, tiled=True)]
    all_to_all x2 -> x0, waiting for transfers between devices: 164 us -> none  [on_device(): lax.all_to_all(partial_value.reshape(devices, count, width), 'expert', sp...]
    all_to_all x2 -> x0, starting transfers between devices: 15.2 us -> none  [on_device(): lax.all_to_all(partial_value.reshape(devices, count, width), 'expert', sp...]
  transfers between devices with their start and end apart: 4 -> 6, of which waited for: 4 -> 6; matrix products, arithmetic and copies ran while one was open for 0% -> 0% of each run, Pallas kernels for 0% -> 0%
where the time goes in v1:
time: 1030 us; the launch traced here: 1020 us
  waiting for transfers between devices  979 us (95%)
  matrix products  13.6 us (1%)
  between operations  13.3 us (1%)
    reduce_scatter x2, waiting for transfers between devices, on_device(): mixed = lax.psum_scatter(partial, 'expert', scatter_dimension=0, tiled=True)  487 us
    all_gather x2, waiting for transfers between devices, on_device(): rows = lax.all_gather(block, 'expert', axis=0, tiled=True)  463 us
    ppermute x2, waiting for transfers between devices, on_device(): lax.ppermute(updated, 'section', [(s, (s + 1) % sections) for s in range(...  28.8 us
  transfers between devices with their start and end apart: 6, of which 6 were waited for; matrix products, arithmetic and copies ran while one was open for 0% of the time, Pallas kernels for 0%

profile of v1, /device:TPU:6, one launch (start us, length us, event | category | flops | bytes accessed | tf_op | source)
XLA Modules:
  0.0 1018.9 jit_solution(9449483282316703503)
XLA Ops:
  6.5 1.0 fusion.61
  7.6 0.7 slice_bitcast_fusion
  8.3 0.8 reduce
  9.1 0.9 fusion.63
  10.0 1.0 fusion.89
  11.1 0.1 copy.14
  11.2 0.6 fusion.75
  11.8 0.0 reduce-scatter.3.cloned.1.call-start
  11.9 231.9 %all-gather.3.cloned.1.call-done = bf16[256,3712]{1,0:T(8,128)(2,1)} async-done(((bf16[8,3712]{1,0:T(8,128)(2,1)}), bf16[256,3712]{1,0:T(8,128)(2,1)}) %all-gather.3.cloned.1.call-update) | async-done | bytes 1900560 | tf_op jit(solution)/shard_map/all_gather | solution.py:41
  243.8 0.9 select_reduce_fusion.1
  244.7 2.4 fusion.6
  247.2 3.9 convolution_convert_fusion.1
  251.1 0.0 all-gather.5.cloned.1.call-start
  251.2 243.5 %reduce-scatter.3.cloned.1.call-done = bf16[8,3584]{1,0:T(8,128)(2,1)} async-done(((bf16[256,3584]{1,0:T(8,128)(2,1)}), bf16[8,3584]{1,0:T(8,128)(2,1)}) %reduce-scatter.3.cloned.1.call-update) | async-done | bytes 57360 | tf_op jit(solution)/shard_map/reduce_scatter | solution.py:51
  494.6 0.8 fusion.64
  495.5 1.9 collective-permute-start
  497.4 14.4 %collective-permute-done = bf16[8,3584]{1,0:T(8,128)(2,1)S(1)} collective-permute-done((bf16[8,3584]{1,0:T(8,128)(2,1)S(1)}, bf16[8,3584]{1,0:T(8,128)(2,1)S(1)}, u32[]{:S(2)}, u32[]{:S(2)}) %collective-permute-start) | collective-permute-done | bytes 57376 | tf_op jit(solution)/shard_map/ppermute | solution.py:53
  511.8 0.1 fusion.67
  511.9 0.1 fusion.69
  512.0 0.2 fusion.90
  512.2 0.1 copy.15
  512.3 0.6 fusion.76
  513.0 0.0 reduce-scatter.5.cloned.1.call-start
  513.0 230.8 %all-gather.5.cloned.1.call-done = bf16[256,3712]{1,0:T(8,128)(2,1)} async-done(((bf16[8,3712]{1,0:T(8,128)(2,1)}), bf16[256,3712]{1,0:T(8,128)(2,1)}) %all-gather.5.cloned.1.call-update) | async-done | bytes 1900560 | tf_op jit(solution)/shard_map/all_gather | solution.py:41
  743.8 0.9 select_reduce_fusion
  744.8 2.1 fusion.2
  746.9 3.9 convolution_convert_fusion
  750.8 243.7 %reduce-scatter.5.cloned.1.call-done = bf16[8,3584]{1,0:T(8,128)(2,1)} async-done(((bf16[256,3584]{1,0:T(8,128)(2,1)}), bf16[8,3584]{1,0:T(8,128)(2,1)}) %reduce-scatter.5.cloned.1.call-update) | async-done | bytes 57360 | tf_op jit(solution)/shard_map/reduce_scatter | solution.py:51
  994.5 0.8 fusion.70
  995.4 1.9 collective-permute-start.1
  997.3 14.4 %collective-permute-done.1 = bf16[8,3584]{1,0:T(8,128)(2,1)S(1)} collective-permute-done((bf16[8,3584]{1,0:T(8,128)(2,1)S(1)}, bf16[8,3584]{1,0:T(8,128)(2,1)S(1)}, u32[]{:S(2)}, u32[]{:S(2)}) %collective-permute-start.1) | collective-permute-done | bytes 57376 | tf_op jit(solution)/shard_map/ppermute | solution.py:53
  1011.7 0.6 copy.17
  (24 shorter events, 0.2 us)
Async XLA Ops:
  6.5 240.6 %copy-start = (bf16[1,128,3584]{2,1,0:T(8,128)(2,1)S(1)}, bf16[1,128,3584]{2,1,0:T(8,128)(2,1)}, u32[]{:S(2)}) copy-start(bf16[1,128,3584]{2,1,0:T(8,128)(2,1)} %param.12) | copy-start | bytes 2752516
  6.5 237.3 %all-gather.3.cloned.1.call-start = ((), (), s32[]{:S(2)}) async-start(), calls=%async_computation.2 | async-start | bytes 1959936 | tf_op jit(solution)/shard_map/all_gather | solution.py:41
  11.0 236.1 %copy-start.1 = (bf16[1,3584,128]{2,1,0:T(8,128)(2,1)S(1)}, bf16[1,3584,128]{2,1,0:T(8,128)(2,1)}, u32[]{:S(2)}) copy-start(bf16[1,3584,128]{2,1,0:T(8,128)(2,1)} %param.11) | copy-start | bytes 2752516
  11.8 482.8 %reduce-scatter.3.cloned.1.call-start = ((), (), s32[]{:S(2)}) async-start(), calls=%async_computation.3 | async-start | bytes 1892352 | tf_op jit(solution)/shard_map/reduce_scatter | solution.py:51
  247.1 247.5 %copy-start.2 = (bf16[1,8,3584]{2,1,0:T(8,128)(2,1)S(1)}, bf16[1,8,3584]{2,1,0:T(8,128)(2,1)}, u32[]{:S(2)}) copy-start(bf16[1,8,3584]{2,1,0:T(8,128)(2,1)} %param.7) | copy-start | bytes 172036
  251.1 260.9 %copy-start.4 = (bf16[1,3584,4]{1,2,0:T(4,128)(2,1)S(1)}, bf16[1,3584,4]{1,2,0:T(4,128)(2,1)}, u32[]{:S(2)}) copy-start(bf16[1,3584,4]{1,2,0:T(4,128)(2,1)} %param.9) | copy-start | bytes 86020
  251.1 493.7 %copy-start.3 = (bf16[1,3584,128]{2,1,0:T(8,128)(2,1)S(1)}, bf16[1,3584,128]{2,1,0:T(8,128)(2,1)}, u32[]{:S(2)}) copy-start(bf16[1,3584,128]{2,1,0:T(8,128)(2,1)} %param.10) | copy-start | bytes 2752516
  251.1 492.7 %all-gather.5.cloned.1.call-start = ((), (), s32[]{:S(2)}) async-start(), calls=%async_computation.4 | async-start | bytes 1959936 | tf_op jit(solution)/shard_map/all_gather | solution.py:41
  495.5 16.3 %collective-permute-start = (bf16[8,3584]{1,0:T(8,128)(2,1)S(1)}, bf16[8,3584]{1,0:T(8,128)(2,1)S(1)}, u32[]{:S(2)}, u32[]{:S(2)}) collective-permute-start(bf16[8,3584]{1,0:T(8,128)(2,1)S(1)} %fusion.64), channel_id=1, source_target_pairs={{0,32},{32,64},{64,96},{96,128},{128,160},{160,192},{192,224},{224... | collective-permute-start | bytes 172040 | tf_op jit(solution)/shard_map/ppermute | solution.py:53
  513.0 481.6 %reduce-scatter.5.cloned.1.call-start = ((), (), s32[]{:S(2)}) async-start(), calls=%async_computation.5 | async-start | bytes 1892352 | tf_op jit(solution)/shard_map/reduce_scatter | solution.py:51
  995.4 16.3 %collective-permute-start.1 = (bf16[8,3584]{1,0:T(8,128)(2,1)S(1)}, bf16[8,3584]{1,0:T(8,128)(2,1)S(1)}, u32[]{:S(2)}, u32[]{:S(2)}) collective-permute-start(bf16[8,3584]{1,0:T(8,128)(2,1)S(1)} %fusion.70), channel_id=1, source_target_pairs={{0,32},{32,64},{64,96},{96,128},{128,160},{160,192},{192,224},{224... | collective-permute-start | bytes 172040 | tf_op jit(solution)/shard_map/ppermute | solution.py:53
Sparse Core Ops, SparseCore 0:
  11.9 231.8 all-gather.2
  251.2 243.3 reduce-scatter.2
  513.1 230.6 all-gather.4
  751.0 243.5 reduce-scatter.4

commit v2 on v1

v2 whole, which is shorter than its diff:
```python
import jax
import jax.numpy as jnp
from jax import lax
from jax.experimental import pallas as pl
from jax.experimental.pallas import tpu as pltpu
from jax.sharding import PartitionSpec as P

TICKS = 2
EPSILON = 1e-06
RING = 4
LINE = 8
SKIP = 2
LANES = 128
MESH = pl.DeviceIdType.MESH


def kernel(
    x_ref, gain_ref, router_ref, routes_ref, gate_ref, lift_ref, down_ref, out_ref,
    state, rows, w_gate, w_lift, w_out, part, near, line_out, line_in, updated, acc,
    load_sem, gl, gs, gr, rs, rr, hop_s, hop_r,
):
    tok, width = x_ref.shape
    experts = router_ref.shape[0]
    hid = gate_ref.shape[1]
    wide = rows.shape[-1]
    me = lax.axis_index("expert")
    sect = lax.axis_index("section")
    sections = lax.axis_size("section")
    x, z = lax.rem(me, RING), lax.div(me, RING)
    nxt, prv = lax.rem(sect + 1, sections), lax.rem(sect + sections - 1, sections)
    mine = lax.div(me, LINE * RING // experts)

    loads = (
        pltpu.make_async_copy(gate_ref, w_gate, load_sem.at[0]),
        pltpu.make_async_copy(lift_ref, w_lift, load_sem.at[1]),
        pltpu.make_async_copy(down_ref, w_out, load_sem.at[2]),
    )
    for load in loads:
        load.start()

    barrier = pltpu.get_barrier_semaphore()
    for d in range(1, RING):
        other = z * RING + lax.rem(x + d, RING)
        pl.semaphore_signal(barrier, inc=1, device_id={"expert": other}, device_id_type=MESH)
    for d in range(1, LINE):
        other = lax.rem(z + d, LINE) * RING + x
        pl.semaphore_signal(barrier, inc=1, device_id={"expert": other}, device_id_type=MESH)
    for other in (nxt, prv):
        pl.semaphore_signal(barrier, inc=1, device_id={"section": other}, device_id_type=MESH)
    state[0] = x_ref[...]
    pl.semaphore_wait(barrier, RING - 1 + LINE - 1 + 2)

    def send(src, dst, ssem, rsem, device):
        return pltpu.make_async_remote_copy(
            src_ref=src, dst_ref=dst, send_sem=ssem, recv_sem=rsem, device_id=device, device_id_type=MESH
        )

    def inside(zb):
        return (zb >= 0) & (zb < LINE)

    def both_sides(k, work):
        for zb in (z - k, z + k):

            @pl.when(inside(zb))
            def _():
                work(zb)

    def tick(t, carry):
        def g_line(side, reach, owner):
            block = rows.at[t, owner, x]
            target = z + (reach if side == 0 else -reach)
            return send(
                block, block, gl.at[t, side * SKIP + reach - 1, owner], gr.at[t, 0, owner], {"expert": target * RING + x}
            )

        def relays(owner, act):
            for side in range(2):
                for reach in range(1, SKIP + 1):
                    away = z - owner if side == 0 else owner - z
                    target = z + (reach if side == 0 else -reach)

                    @pl.when((away >= 0) & (lax.rem(away + 8 * SKIP, SKIP) == 0) & inside(target))
                    def _():
                        act(g_line(side, reach, owner))

        def g_ring(d, zb, owner):
            block = rows.at[t, zb, owner]
            return send(block, block, gs.at[t, d, zb], gr.at[t, d, zb], {"expert": z * RING + lax.rem(x + d, RING)})

        values = state[t].astype(jnp.float32)
        meansq = jnp.mean(values * values, axis=-1, keepdims=True)
        normed = (values * lax.rsqrt(meansq + EPSILON) * gain_ref[...]).astype(jnp.bfloat16)
        rows[t, z, x, :, pl.ds(0, width)] = normed
        normed = normed.astype(jnp.float32)
        square = (tok, tok)
        same = lax.broadcasted_iota(jnp.int32, square, 0) == lax.broadcasted_iota(jnp.int32, square, 1)
        ids = [
            jnp.sum(jnp.where(same, jnp.broadcast_to(picks, square), 0.0), axis=1, keepdims=True)
            for picks in (routes_ref[t, k : k + 1, :].astype(jnp.float32) for k in range(routes_ref.shape[1]))
        ]
        chosen = []
        for e in range(experts):
            logit = jnp.sum(normed * router_ref[e : e + 1, :].astype(jnp.float32), axis=1, keepdims=True)
            named = sum(jnp.where(one == e, 1.0, 0.0) for one in ids)
            chosen.append(named * jax.nn.sigmoid(logit))
        total = sum(chosen[1:], chosen[0])
        lane = lax.broadcasted_iota(jnp.int32, (tok, LANES), 1)
        extra = jnp.zeros((tok, LANES), jnp.float32)
        for e in range(experts):
            gate = chosen[e] / total
            high = gate.astype(jnp.bfloat16).astype(jnp.float32)
            extra = jnp.where(lane == e, high, extra)
            extra = jnp.where(lane == experts + e, gate - high, extra)
        rows[t, z, x, :, pl.ds(width, LANES)] = extra.astype(jnp.bfloat16)

        def ring_sends(zb):
            for d in range(1, RING):
                g_ring(d, zb, x).start()

        def line_arrived(zb):
            g_line(0, 1, zb).wait_recv()
            relays(zb, lambda copy: copy.start())
            ring_sends(zb)

        def ring_arrived(zb, carry):
            for d in range(1, RING):
                g_ring(d, zb, lax.rem(x + RING - d, RING)).wait_recv()
            return carry

        def outward(first, work):
            def one(k, carry):
                both_sides(k, work)
                return carry

            lax.fori_loop(first, LINE, one, 0)

        relays(z, lambda copy: copy.start())
        ring_sends(z)
        outward(1, line_arrived)
        lax.fori_loop(0, LINE, ring_arrived, 0)

        @pl.when(t == 0)
        def _():
            for load in loads:
                load.wait()

        flat = rows[t].reshape(LINE * RING * tok, wide)
        lane = lax.broadcasted_iota(jnp.int32, (LINE * RING * tok, LANES), 1)
        extra = flat[:, width:].astype(jnp.float32)
        weight = jnp.sum(
            jnp.where((lane == mine) | (lane == mine + experts), extra, 0.0), axis=1, keepdims=True
        )
        w_in = jnp.concatenate([w_gate[...], w_lift[...]], axis=1)
        both = jnp.dot(flat[:, :width], w_in, preferred_element_type=jnp.float32)
        gate_out, lifted = both[:, :hid], both[:, hid:]
        hidden = (gate_out / (1.0 + jnp.exp(-gate_out)) * lifted * weight).astype(jnp.bfloat16)
        span = 512
        for c in range(width // span):
            cols = pl.ds(c * span, span)
            made = jnp.dot(hidden, w_out[:, cols], preferred_element_type=jnp.float32)
            part[t, :, :, :, cols] = made.astype(jnp.bfloat16).reshape(LINE, RING, tok, span)

        def r_ring(d, zb):
            other = lax.rem(x + d, RING)
            return send(
                part.at[t, zb, other], near.at[t, d - 1, zb], rs.at[t, d, zb], rr.at[t, d, zb], {"expert": z * RING + other}
            )

        def r_line(zb, owner):
            return send(
                line_out.at[t, zb], line_in.at[t, owner], rs.at[t, 0, zb], rr.at[t, 0, owner], {"expert": zb * RING + x}
            )

        def ring_reduce(zb):
            for d in range(1, RING):
                r_ring(d, zb).start()

        def ring_sum(zb):
            total = part[t, zb, x].astype(jnp.float32)
            for d in range(1, RING):
                r_ring(d, zb).wait_recv()
                total = total + near[t, d - 1, zb].astype(jnp.float32)
            return total

        def line_reduce(zb):
            line_out[t, zb] = ring_sum(zb).astype(jnp.bfloat16)
            r_line(zb, z).start()

        def line_sum(zb):
            r_line(z, zb).wait_recv()
            acc[...] += line_in[t, zb].astype(jnp.float32)

        def inward(work):
            def one(i, carry):
                both_sides(LINE - 1 - i, work)
                return carry

            lax.fori_loop(0, LINE - 1, one, 0)

        inward(ring_reduce)
        ring_reduce(z)
        inward(line_reduce)
        acc[...] = ring_sum(z) + state[t].astype(jnp.float32)
        inward(line_sum)
        updated[t] = acc[...].astype(jnp.bfloat16)
        hop = send(updated.at[t], state.at[t + 1], hop_s.at[t], hop_r.at[t], {"section": nxt})
        hop.start()

        def finish(zb, carry):
            for d in range(1, RING):
                g_ring(d, zb, x).wait_send()
                r_ring(d, zb).wait_send()

            @pl.when(zb != z)
            def _():
                r_line(zb, z).wait_send()

            relays(zb, lambda copy: copy.wait_send())
            return carry

        lax.fori_loop(0, LINE, finish, 0)
        hop.wait_recv()
        hop.wait_send()
        return carry

    lax.fori_loop(0, TICKS, tick, 0)
    out_ref[...] = state[TICKS]


def on_device(states, norm_gain, router, w_gate, w_up, w_down, routes):
    tok, width = states.shape[1:]
    hid = w_gate.shape[2]
    vmem, hbm = pl.BlockSpec(memory_space=pltpu.VMEM), pl.BlockSpec(memory_space=pl.ANY)
    half = jnp.bfloat16
    made = pl.pallas_call(
        kernel,
        out_shape=jax.ShapeDtypeStruct((tok, width), half),
        in_specs=[vmem, vmem, vmem, vmem, hbm, hbm, hbm],
        out_specs=vmem,
        scratch_shapes=[
            pltpu.VMEM((TICKS + 1, tok, width), half),
            pltpu.VMEM((TICKS, LINE, RING, tok, width + LANES), half),
            pltpu.VMEM((width, hid), half),
            pltpu.VMEM((width, hid), half),
            pltpu.VMEM((hid, width), half),
            pltpu.VMEM((TICKS, LINE, RING, tok, width), half),
            pltpu.VMEM((TICKS, RING - 1, LINE, tok, width), half),
            pltpu.VMEM((TICKS, LINE, tok, width), half),
            pltpu.VMEM((TICKS, LINE, tok, width), half),
            pltpu.VMEM((TICKS, tok, width), half),
            pltpu.VMEM((tok, width), jnp.float32),
            pltpu.SemaphoreType.DMA((3,)),
            pltpu.SemaphoreType.DMA((TICKS, 2 * SKIP, LINE)),
            pltpu.SemaphoreType.DMA((TICKS, RING, LINE)),
            pltpu.SemaphoreType.DMA((TICKS, RING, LINE)),
            pltpu.SemaphoreType.DMA((TICKS, RING, LINE)),
            pltpu.SemaphoreType.DMA((TICKS, RING, LINE)),
            pltpu.SemaphoreType.DMA((TICKS,)),
            pltpu.SemaphoreType.DMA((TICKS,)),
        ],
        compiler_params=pltpu.CompilerParams(
            collective_id=0, has_side_effects=True, vmem_limit_bytes=56 * 2**20
        ),
    )(
        states[0],
        norm_gain,
        jnp.transpose(router[0]),
        jnp.transpose(routes[:, 0], (0, 2, 1)),
        w_gate[0],
        w_up[0],
        w_down[0],
    )
    return made[None]


def solution(mesh):
    placed = (
        P("section", "expert", None),
        P("section", None),
        P("section", None, None),
        P("section", None, "expert"),
        P("section", None, "expert"),
        P("section", "expert", None),
        P(None, "section", "expert", None),
    )
    return jax.shard_map(
        on_device,
        mesh=mesh,
        in_specs=placed,
        out_specs=P("section", "expert", None),
        check_vma=False,
    )
```

time: 1030 us -> 137 us (0.13)
  waiting for transfers between devices: 979 us -> 0 us
  Pallas kernels: 0 us -> 133 us
  matrix products: 13.6 us -> 0 us
  between operations: 13.3 us -> 0.01 us
    reduce_scatter x2 -> x0, waiting for transfers between devices: 487 us -> none  [on_device(): mixed = lax.psum_scatter(partial, 'expert', scatter_dimension=0, tiled=True)]
    all_gather x2 -> x0, waiting for transfers between devices: 463 us -> none  [on_device(): rows = lax.all_gather(block, 'expert', axis=0, tiled=True)]
    pallas_call x0 -> x1, Pallas kernels: none -> 133 us  [on_device(): pl.pallas_call(kernel, out_shape=jax.ShapeDtypeStruct((tok, width), half)...]
    ppermute x2 -> x0, waiting for transfers between devices: 28.8 us -> none  [on_device(): lax.ppermute(updated, 'section', [(s, (s + 1) % sections) for s in range(...]
    dot_general x6 -> x0, matrix products: 13.6 us -> none  [the longest x2 7.84 us: on_device(): jnp.dot(hidden, w_down[0], preferred_element_type=jnp.float32)]
  transfers between devices with their start and end apart: 6 -> 0, of which waited for: 6 -> 0; matrix products, arithmetic and copies ran while one was open for 0% -> 0% of each run, Pallas kernels for 0% -> 0%
where the time goes in v2:
time: 137 us; the launch traced here: 135 us
  Pallas kernels  133 us (97%)
  local copies, waits for them, and re-layouts  1.45 us (1%)
    pallas_call x1, Pallas kernels, on_device(): pl.pallas_call(kernel, out_shape=jax.ShapeDtypeStruct((tok, width), half)...  133 us

profile of v2, /device:TPU:6, one launch (start us, length us, event | category | flops | bytes accessed | tf_op | source)
XLA Modules:
  0.0 134.8 jit_solution(13965334670037054095)
XLA Ops:
  0.0 133.4 %shard_map.73 = bf16[8,3584]{1,0:T(8,128)(2,1)} custom-call(bf16[8,3584]{1,0:T(8,128)(2,1)} %bitcast.15, f32[1,3584]{1,0:T(1,128)} %gain_ref.1, bf16[4,3584]{1,0:T(4,128)(2,1)} %bitcast.16, s32[2,2,8]{2,1,0:T(2,128)} %bitcast.17, bf16[3584,128]{1,0:T(8,128)(2,1)} %bitcast.11, bf16[3584,128]{1,0:T(8,128)(2,1)} %bitcast.12, bf16[128,3584]{1,0:T(8,128)(2,1)} %bitcast.13), custom_call_target="tpu_custom_call" | custom-call | tf_op jit(solution)/shard_map/pallas_call | solution.py:235
  133.4 1.4 %copy.9 = bf16[1,8,3584]{2,1,0:T(8,128)(2,1)} copy(bf16[1,8,3584]{2,1,0:T(8,128)(2,1)} %bitcast.14) | data formatting | bytes 114688

commit v3 on v2

--- a/solution.py
+++ b/solution.py
@@ -9,6 +9,7 @@
 EPSILON = 1e-06
 RING = 4
 LINE = 8
+FIRST = 4
 SKIP = 2
 LANES = 128
 MESH = pl.DeviceIdType.MESH
@@ -17,12 +18,13 @@
 def kernel(
     x_ref, gain_ref, router_ref, routes_ref, gate_ref, lift_ref, down_ref, out_ref,
     state, rows, w_gate, w_lift, w_out, part, near, line_out, line_in, updated, acc,
-    load_sem, gl, gs, gr, rs, rr, hop_s, hop_r,
+    load_sem, frs, frr, fls, flr, gl, gs, gr, rs, rr, hop_s, hop_r,
 ):
     tok, width = x_ref.shape
     experts = router_ref.shape[0]
     hid = gate_ref.shape[1]
     wide = rows.shape[-1]
+    first = FIRST * LANES
     me = lax.axis_index("expert")
     sect = lax.axis_index("section")
     sections = lax.axis_size("section")
@@ -67,13 +69,13 @@
 
     def tick(t, carry):
         def g_line(side, reach, owner):
-            block = rows.at[t, owner, x]
+            block = rows.at[t, owner, x, :, pl.ds(first, wide - first)]
             target = z + (reach if side == 0 else -reach)
             return send(
                 block, block, gl.at[t, side * SKIP + reach - 1, owner], gr.at[t, 0, owner], {"expert": target * RING + x}
             )
 
-        def relays(owner, act):
+        def relays(owner, act, make=g_line):
             for side in range(2):
                 for reach in range(1, SKIP + 1):
                     away = z - owner if side == 0 else owner - z
@@ -81,10 +83,36 @@
 
                     @pl.when((away >= 0) & (lax.rem(away + 8 * SKIP, SKIP) == 0) & inside(target))
                     def _():
-                        act(g_line(side, reach, owner))
+                        act(make(side, reach, owner))
+
+        def f_ring(d, owner):
+            block = rows.at[t, z, owner, :, pl.ds(0, first)]
+            device = {"expert": z * RING + lax.rem(x + d, RING)}
+            return send(block, block, frs.at[t, d], frr.at[t, d], device)
+
+        def f_line(column):
+            def make(side, reach, owner):
+                block = rows.at[t, owner, column, :, pl.ds(0, first)]
+                target = z + (reach if side == 0 else -reach)
+                slot = column * 2 * SKIP + side * SKIP + reach - 1
+                device = {"expert": target * RING + x}
+                return send(block, block, fls.at[t, slot, owner], flr.at[t, column, owner], device)
+
+            return make
+
+        def f_relays(owner, column, act):
+            relays(owner, act, f_line(column))
+
+        def f_arrived(zb):
+            def one(column, carry):
+                f_line(column)(0, 1, zb).wait_recv()
+                f_relays(zb, column, lambda copy: copy.start())
+                return carry
+
+            lax.fori_loop(0, RING, one, 0)
 
         def g_ring(d, zb, owner):
-            block = rows.at[t, zb, owner]
+            block = rows.at[t, zb, owner, :, pl.ds(first, wide - first)]
             return send(block, block, gs.at[t, d, zb], gr.at[t, d, zb], {"expert": z * RING + lax.rem(x + d, RING)})
 
         values = state[t].astype(jnp.float32)
@@ -135,8 +163,24 @@
             lax.fori_loop(first, LINE, one, 0)
 
         relays(z, lambda copy: copy.start())
+        for d in (1, 3, 2):
+            f_ring(d, x).start()
+        f_relays(z, x, lambda copy: copy.start())
         ring_sends(z)
-        outward(1, line_arrived)
+        for d in (1, 3, 2):
+            f_ring(d, lax.rem(x + RING - d, RING)).wait_recv()
+            f_relays(z, lax.rem(x + RING - d, RING), lambda copy: copy.start())
+
+        def arrivals(k, carry):
+            both_sides(k, line_arrived)
+
+            @pl.when(k > 1)
+            def _():
+                both_sides(k - 1, f_arrived)
+
+            return carry
+
+        lax.fori_loop(1, LINE + 1, arrivals, 0)
         lax.fori_loop(0, LINE, ring_arrived, 0)
 
         @pl.when(t == 0)
@@ -199,6 +243,23 @@
 
         inward(ring_reduce)
         ring_reduce(z)
+
+        def gathered(zb, carry):
+            for d in range(1, RING):
+                g_ring(d, zb, x).wait_send()
+
+            relays(zb, lambda copy: copy.wait_send())
+
+            def columns(column, carry):
+                f_relays(zb, column, lambda copy: copy.wait_send())
+                return carry
+
+            lax.fori_loop(0, RING, columns, 0)
+            return carry
+
+        lax.fori_loop(0, LINE, gathered, 0)
+        for d in range(1, RING):
+            f_ring(d, x).wait_send()
         inward(line_reduce)
         acc[...] = ring_sum(z) + state[t].astype(jnp.float32)
         inward(line_sum)
@@ -208,14 +269,12 @@
 
         def finish(zb, carry):
             for d in range(1, RING):
-                g_ring(d, zb, x).wait_send()
                 r_ring(d, zb).wait_send()
 
             @pl.when(zb != z)
             def _():
                 r_line(zb, z).wait_send()
 
-            relays(zb, lambda copy: copy.wait_send())
             return carry
 
         lax.fori_loop(0, LINE, finish, 0)
@@ -250,6 +309,10 @@
             pltpu.VMEM((TICKS, tok, width), half),
             pltpu.VMEM((tok, width), jnp.float32),
             pltpu.SemaphoreType.DMA((3,)),
+            pltpu.SemaphoreType.DMA((TICKS, RING)),
+            pltpu.SemaphoreType.DMA((TICKS, RING)),
+            pltpu.SemaphoreType.DMA((TICKS, RING * 2 * SKIP, LINE)),
+            pltpu.SemaphoreType.DMA((TICKS, RING, LINE)),
             pltpu.SemaphoreType.DMA((TICKS, 2 * SKIP, LINE)),
             pltpu.SemaphoreType.DMA((TICKS, RING, LINE)),
             pltpu.SemaphoreType.DMA((TICKS, RING, LINE)),

time: 137 us -> 135 us (0.985)
  no operation moved by 1% of the time
where the time goes in v3:
time: 135 us; the launch traced here: 134 us
  Pallas kernels  132 us (98%)
  local copies, waits for them, and re-layouts  1.45 us (1%)
    pallas_call x1, Pallas kernels, on_device(): pl.pallas_call(kernel, out_shape=jax.ShapeDtypeStruct((tok, width), half)...  132 us

profile of v3, /device:TPU:6, one launch (start us, length us, event | category | flops | bytes accessed | tf_op | source)
XLA Modules:
  0.0 133.5 jit_solution(610536523524804131)
XLA Ops:
  0.0 132.1 %shard_map.73 = bf16[8,3584]{1,0:T(8,128)(2,1)} custom-call(bf16[8,3584]{1,0:T(8,128)(2,1)} %bitcast.15, f32[1,3584]{1,0:T(1,128)} %gain_ref.1, bf16[4,3584]{1,0:T(4,128)(2,1)} %bitcast.16, s32[2,2,8]{2,1,0:T(2,128)} %bitcast.17, bf16[3584,128]{1,0:T(8,128)(2,1)} %bitcast.11, bf16[3584,128]{1,0:T(8,128)(2,1)} %bitcast.12, bf16[128,3584]{1,0:T(8,128)(2,1)} %bitcast.13), custom_call_target="tpu_custom_call" | custom-call | tf_op jit(solution)/shard_map/pallas_call | solution.py:294
  132.1 1.4 %copy.9 = bf16[1,8,3584]{2,1,0:T(8,128)(2,1)} copy(bf16[1,8,3584]{2,1,0:T(8,128)(2,1)} %bitcast.14) | data formatting | bytes 114688

commit v4 on v3

--- a/solution.py
+++ b/solution.py
@@ -29,6 +29,7 @@
     sect = lax.axis_index("section")
     sections = lax.axis_size("section")
     x, z = lax.rem(me, RING), lax.div(me, RING)
+    ring_next = {"expert": z * RING + lax.rem(x + 1, RING)}
     nxt, prv = lax.rem(sect + 1, sections), lax.rem(sect + sections - 1, sections)
     mine = lax.div(me, LINE * RING // experts)
 
@@ -37,9 +38,6 @@
         pltpu.make_async_copy(lift_ref, w_lift, load_sem.at[1]),
         pltpu.make_async_copy(down_ref, w_out, load_sem.at[2]),
     )
-    for load in loads:
-        load.start()
-
     barrier = pltpu.get_barrier_semaphore()
     for d in range(1, RING):
         other = z * RING + lax.rem(x + d, RING)
@@ -49,6 +47,8 @@
         pl.semaphore_signal(barrier, inc=1, device_id={"expert": other}, device_id_type=MESH)
     for other in (nxt, prv):
         pl.semaphore_signal(barrier, inc=1, device_id={"section": other}, device_id_type=MESH)
+    for load in loads:
+        load.start()
     state[0] = x_ref[...]
     pl.semaphore_wait(barrier, RING - 1 + LINE - 1 + 2)
 
@@ -105,7 +105,8 @@
 
         def f_arrived(zb):
             def one(column, carry):
-                f_line(column)(0, 1, zb).wait_recv()
+                block = rows.at[t, zb, column, :, pl.ds(0, first)]
+                send(block, block, fls.at[t, 0, zb], flr.at[t, column, zb], ring_next).wait_recv()
                 f_relays(zb, column, lambda copy: copy.start())
                 return carry
 
@@ -146,7 +147,8 @@
                 g_ring(d, zb, x).start()
 
         def line_arrived(zb):
-            g_line(0, 1, zb).wait_recv()
+            block = rows.at[t, zb, x, :, pl.ds(first, wide - first)]
+            send(block, block, gl.at[t, 0, zb], gr.at[t, 0, zb], ring_next).wait_recv()
             relays(zb, lambda copy: copy.start())
             ring_sends(zb)
 

time: 135 us -> 134 us (level)
  no operation moved by 1% of the time
where the time goes in v4:
time: 134 us; the launch traced here: 132 us
  Pallas kernels  131 us (98%)
  local copies, waits for them, and re-layouts  1.45 us (1%)
    pallas_call x1, Pallas kernels, on_device(): pl.pallas_call(kernel, out_shape=jax.ShapeDtypeStruct((tok, width), half)...  131 us

profile of v4, /device:TPU:6, one launch (start us, length us, event | category | flops | bytes accessed | tf_op | source)
XLA Modules:
  0.0 132.3 jit_solution(9867485852466766928)
XLA Ops:
  0.0 130.8 %shard_map.73 = bf16[8,3584]{1,0:T(8,128)(2,1)} custom-call(bf16[8,3584]{1,0:T(8,128)(2,1)} %bitcast.15, f32[1,3584]{1,0:T(1,128)} %gain_ref.1, bf16[4,3584]{1,0:T(4,128)(2,1)} %bitcast.16, s32[2,2,8]{2,1,0:T(2,128)} %bitcast.17, bf16[3584,128]{1,0:T(8,128)(2,1)} %bitcast.11, bf16[3584,128]{1,0:T(8,128)(2,1)} %bitcast.12, bf16[128,3584]{1,0:T(8,128)(2,1)} %bitcast.13), custom_call_target="tpu_custom_call" | custom-call | tf_op jit(solution)/shard_map/pallas_call | solution.py:296
  130.8 1.4 %copy.9 = bf16[1,8,3584]{2,1,0:T(8,128)(2,1)} copy(bf16[1,8,3584]{2,1,0:T(8,128)(2,1)} %bitcast.14) | data formatting | bytes 114688
